TPU v7x, 32 devices: a whole 2x2x4 slice. The times are simulated.
32 devices in a mesh: vel: 2 (over y), cell: 16 (over z, x, core).
Axes of the slice: x: 2, y: 2, z: 4, core: 2. Of those that a mesh axis runs over, the one named last changes fastest.
Arguments:
- distribution: float32 [4096, 4096], P('vel', 'cell'), as said below
- cell_count: int32 [16], P('cell'), may hold values from 192 to 256, as said below
- cell_level: int32 [4096], P('cell'), may hold values from 0 to 1
- send_list: int32 [4, 1024], P(None, 'cell'), may hold values from 0 to 255, as said below
- face_neighbour: int32 [6, 4096], P(None, 'cell'), may hold values from 0 to 511
- face_level: int32 [6, 4096], P(None, 'cell'), may hold values from 0 to 1
Outputs:
- advanced: float32 [4096, 4096], P('vel', 'cell')
Inputs may be any that keep to these rules, and one draw needn't show every extreme that they name: The live cells of index d of cell are its slots 0 to cell_count[d] - 1; the rest are padding. Some index has all 256 live. `send_list`: row k of index d lists live local cells of d; the neighbour d + o_k, o = (-2, -1, 1, 2), reads a prefix of the row, and no one reads a row toward an index outside the mesh. Every index has some row whose 64 slots are all read. `distribution`: positive everywhere.
All inputs are finite; a program needn't handle non-finite values.
Results may differ from a plain program's by a relative error of at most 0.0001.
Values sent between devices are 32-bit elements; how exact they have to be, the bound alone decides.
A program may use at most 64 MiB of HBM per device.

v0:
```python
import math

import jax
import jax.numpy as jnp
from jax import lax
from jax.sharding import PartitionSpec as P

NV = 16
STEPS = 2


speed_limit = 5.0
time_step = 0.03
nominal_shear_drag = 0.5
power_law_index = 0.81
conduction_quotient = 2.0 / 3.0


def from_behind(block, axis, distance):
    devices = range(lax.axis_size(axis))
    route = [(i - distance, i) for i in devices if i - distance in devices]
    return lax.ppermute(block, axis, route)


def grid_speeds(first, count):
    index = first + jnp.arange(count, dtype=jnp.int32)
    spacing = 2.0 * speed_limit / NV
    lattice_nodes_east = -speed_limit + ((index // (NV * NV)).astype(jnp.float32) + 0.5) * spacing
    lattice_nodes_north = -speed_limit + ((index // NV % NV).astype(jnp.float32) + 0.5) * spacing
    lattice_nodes_upward = -speed_limit + ((index % NV).astype(jnp.float32) + 0.5) * spacing
    return (
        lattice_nodes_east[:, None],
        lattice_nodes_north[:, None],
        lattice_nodes_upward[:, None],
    )


def quadrature_weight():
    return (2.0 * speed_limit / NV) ** 3 * (2.0 * math.pi) ** (-1.5)


def face_ratios(cell_level, face_level):
    own_level = cell_level[None, :]
    coarser = jnp.maximum(own_level, face_level)
    return jnp.exp2((3 * own_level - 2 * coarser).astype(jnp.float32))


def invariant_integrals(
    local_concentration, moment_x, moment_y, moment_z, complete_enthalpy_sum, occupied_flags
):
    safe_positive_entry = jnp.where(occupied_flags, local_concentration, 1.0)
    mean_flow_east = moment_x / safe_positive_entry
    mean_flow_north = moment_y / safe_positive_entry
    mean_flow_upward = moment_z / safe_positive_entry
    kinetic_warmth = jnp.where(
        occupied_flags,
        (
            complete_enthalpy_sum / safe_positive_entry
            - (
                mean_flow_east * mean_flow_east
                + mean_flow_north * mean_flow_north
                + mean_flow_upward * mean_flow_upward
            )
        )
        / 3.0,
        1.0,
    )
    return (safe_positive_entry, mean_flow_east, mean_flow_north, mean_flow_upward, kinetic_warmth)


def corrected_profile(
    lattice_nodes_east,
    lattice_nodes_north,
    lattice_nodes_upward,
    local_concentration,
    mean_flow_vectors,
    kinetic_warmth,
    isotropic_stress,
    conduction_vectors,
):
    width_east = lattice_nodes_east - mean_flow_vectors[0][None, :]
    width_north = lattice_nodes_north - mean_flow_vectors[1][None, :]
    width_upward = lattice_nodes_upward - mean_flow_vectors[2][None, :]
    agitation_magnitude = (
        width_east * width_east + width_north * width_north + width_upward * width_upward
    )
    gaussian_profile = (local_concentration * kinetic_warmth ** (-1.5))[None, :] * jnp.exp(
        -agitation_magnitude / (2.0 * kinetic_warmth[None, :])
    )
    coordinate_location = (
        width_east * conduction_vectors[0][None, :]
        + width_north * conduction_vectors[1][None, :]
        + width_upward * conduction_vectors[2][None, :]
    )
    multiplier_coefficient = (1.0 - conduction_quotient) / (5.0 * isotropic_stress * kinetic_warmth)
    return gaussian_profile * (
        1.0
        + multiplier_coefficient[None, :]
        * coordinate_location
        * (agitation_magnitude / kinetic_warmth[None, :] - 5.0)
    )


def integral_entries(
    state_values, lattice_nodes_east, lattice_nodes_north, lattice_nodes_upward, occupied_flags
):
    quadrature = quadrature_weight()
    ones = jnp.ones_like(lattice_nodes_east)
    squared = (
        lattice_nodes_east * lattice_nodes_east
        + lattice_nodes_north * lattice_nodes_north
        + lattice_nodes_upward * lattice_nodes_upward
    )
    matrix = (
        quadrature
        * jnp.concatenate(
            [ones, lattice_nodes_east, lattice_nodes_north, lattice_nodes_upward, squared], axis=1
        ).T
    )
    integral_sums = lax.psum(jnp.dot(matrix, state_values, precision=lax.Precision.HIGHEST), "vel")
    local_concentration = integral_sums[0]
    safe_positive_entry, mean_flow_east, mean_flow_north, mean_flow_upward, kinetic_warmth = (
        invariant_integrals(
            local_concentration,
            integral_sums[1],
            integral_sums[2],
            integral_sums[3],
            integral_sums[4],
            occupied_flags,
        )
    )
    width_east = lattice_nodes_east - mean_flow_east[None, :]
    width_north = lattice_nodes_north - mean_flow_north[None, :]
    width_upward = lattice_nodes_upward - mean_flow_upward[None, :]
    scaled = (
        0.5
        * quadrature
        * (width_east * width_east + width_north * width_north + width_upward * width_upward)
        * state_values
    )
    partial_heat = jnp.stack(
        [
            jnp.sum(width_east * scaled, 0),
            jnp.sum(width_north * scaled, 0),
            jnp.sum(width_upward * scaled, 0),
        ]
    )
    summed = lax.psum(partial_heat, "vel")
    conduction_vectors = (summed[0], summed[1], summed[2])
    return (
        local_concentration,
        safe_positive_entry,
        (mean_flow_east, mean_flow_north, mean_flow_upward),
        kinetic_warmth,
        conduction_vectors,
    )


def ghost_columns(state_values, send_list):
    received = []
    for group_id, offset in enumerate((-2, -1, 1, 2)):
        packet = jnp.take(state_values, send_list[3 - group_id], axis=1)
        received.append(from_behind(packet, "cell", -offset))
    return jnp.concatenate([state_values] + received, axis=1)


def advance(
    state_values,
    lattice_nodes_east,
    lattice_nodes_north,
    lattice_nodes_upward,
    occupied_flags,
    normalized_peculiar,
    send_list,
    face_neighbour,
):
    (
        local_concentration,
        safe_positive_entry,
        mean_flow_vectors,
        kinetic_warmth,
        conduction_vectors,
    ) = integral_entries(
        state_values, lattice_nodes_east, lattice_nodes_north, lattice_nodes_upward, occupied_flags
    )
    isotropic_stress = safe_positive_entry * kinetic_warmth
    inverse_relax_time = isotropic_stress / (nominal_shear_drag * kinetic_warmth**power_law_index)
    extended = ghost_columns(state_values, send_list)
    balance_profile = corrected_profile(
        lattice_nodes_east,
        lattice_nodes_north,
        lattice_nodes_upward,
        local_concentration,
        mean_flow_vectors,
        kinetic_warmth,
        isotropic_stress,
        conduction_vectors,
    )
    flux = jnp.zeros_like(state_values)
    speeds = (lattice_nodes_east, lattice_nodes_north, lattice_nodes_upward)
    for face_slot in range(6):
        normal = speeds[face_slot // 2] * (1.0 - 2.0 * (face_slot % 2))
        across = jnp.take(extended, face_neighbour[face_slot], axis=1)
        flux = flux + normalized_peculiar[face_slot][None, :] * (
            jnp.maximum(normal, 0.0) * state_values + jnp.minimum(normal, 0.0) * across
        )
    refreshed_distribution = (
        state_values
        - time_step * flux
        + time_step * inverse_relax_time[None, :] * (balance_profile - state_values)
    )
    return jnp.where(occupied_flags[None, :], refreshed_distribution, 0.0)


def body(distribution, cell_count, cell_level, send_list, face_neighbour, face_level):
    vel_rows, cell_slots = distribution.shape
    lattice_nodes_east, lattice_nodes_north, lattice_nodes_upward = grid_speeds(
        lax.axis_index("vel") * vel_rows, vel_rows
    )
    occupied_flags = jnp.arange(cell_slots, dtype=jnp.int32) < cell_count[0]
    normalized_peculiar = face_ratios(cell_level, face_level)
    state_values = distribution
    for step_number in range(STEPS):
        state_values = advance(
            state_values,
            lattice_nodes_east,
            lattice_nodes_north,
            lattice_nodes_upward,
            occupied_flags,
            normalized_peculiar,
            send_list,
            face_neighbour,
        )
    return state_values


def solution(mesh):
    placed = (
        P("vel", "cell"),
        P("cell"),
        P("cell"),
        P(None, "cell"),
        P(None, "cell"),
        P(None, "cell"),
    )
    return jax.shard_map(
        body, mesh=mesh, in_specs=placed, out_specs=P("vel", "cell"), check_vma=False
    )
```

profile of v0, /device:TPU:0, one launch (start us, length us, event | category | flops | bytes accessed | tf_op | source)
XLA Modules:
  0.0 208.2 jit_solution(13538973165282438160)
XLA Ops:
  0.9 1.9 copy.33
  3.6 0.9 select_bitcast_fusion.4
  4.5 1.3 collective-permute-start.3
  6.5 0.9 select_bitcast_fusion.7
  7.4 6.3 %collective-permute-start = (f32[2048,64]{0,1:T(8,128)}, f32[2048,64]{0,1:T(8,128)}, u32[]{:S(2)}, u32[]{:S(2)}) collective-permute-start(f32[2048,64]{0,1:T(8,128)} %select_bitcast_fusion.7), channel_id=1, source_target_pairs={{0,2},{1,3},{2,4},{3,5},{4,6},{5,7},{6,8},{7,9},{8,10},{9,11},{10,... | collective-permute-start | bytes 1572872 | tf_op jit(solution)/shard_map/ppermute | solution.py:22
  14.5 0.9 select_bitcast_fusion.6
  15.4 2.3 %collective-permute-start.1 = (f32[2048,64]{0,1:T(8,128)}, f32[2048,64]{0,1:T(8,128)}, u32[]{:S(2)}, u32[]{:S(2)}) collective-permute-start(f32[2048,64]{0,1:T(8,128)} %select_bitcast_fusion.6), channel_id=1, source_target_pairs={{0,1},{1,2},{2,3},{3,4},{4,5},{5,6},{6,7},{7,8},{8,9},{9,10},{10,1... | collective-permute-start | bytes 1572872 | tf_op jit(solution)/shard_map/ppermute | solution.py:22
  18.4 0.9 select_bitcast_fusion.5
  19.4 1.3 collective-permute-start.2
  22.1 2.5 %fusion.86 = f32[5,256]{1,0:T(8,128)S(1)} fusion(f32[2048,256]{1,0:T(8,128)} %param.10, f32[2048,5]{0,1:T(8,128)S(1)} %concatenate.11), kind=kOutput, calls=%fused_computation.144 | convolution fusion | flops 31467520 | bytes 2143232 | tf_op jit(solution)/shard_map/dot_general | solution.py:120
  24.6 5.0 %psum.28 = f32[5,256]{1,0:T(8,128)S(1)} all-reduce(f32[5,256]{1,0:T(8,128)S(1)} %fusion.86), channel_id=1, replica_groups=mesh['vel'=2,'cell'=16] {'vel'}, use_global_device_ids=true, to_apply=%region_0.3 | all-reduce | flops 1280 | bytes 10240 | tf_op jit(solution)/shard_map/psum | solution.py:120
  29.6 2.1 %constant_dynamic-update-slice_fusion.4 = (f32[2048,512]{0,1:T(8,128)}, f32[2048,256]{0,1:T(8,128)S(1)}) fusion(f32[2048,256]{0,1:T(8,128)S(1)} %copy.33, f32[256]{0:T(256)S(1)} %bitcast.212, f32[2048]{0:T(1024)S(1)} %fusion.103, f32[256]{0:T(256)S(1)} %bitcast.209, f32[2048]{0:T(1024)S(1)} %get-tuple-element.66, f32[256]{0:T(256)S(1)} %bitcast.206, ...), kind=kLoop, calls=%fused_computation.158 | loop fusion | flops 5242879 | bytes 6319104
  32.5 5.2 %psum.29 = f32[3,256]{1,0:T(4,128)S(1)} all-reduce(f32[3,256]{1,0:T(4,128)S(1)} %pad_maximum_fusion), channel_id=1, replica_groups=mesh['vel'=2,'cell'=16] {'vel'}, use_global_device_ids=true, to_apply=%region_4.7 | all-reduce | flops 768 | bytes 6144 | tf_op jit(solution)/shard_map/psum | solution.py:148
  38.6 1.9 constant_dynamic-update-slice_fusion.3
  40.5 1.9 constant_dynamic-update-slice_fusion.2
  42.4 1.9 constant_dynamic-update-slice_fusion.1
  45.1 5.8 %gather_fusion.9 = f32[256,2048]{1,0:T(8,128)} fusion(f32[2048,512]{0,1:T(8,128)} %constant_dynamic-update-slice_fusion, s32[1024]{0:T(1024)S(1)} %get-tuple-element.83), kind=kCustom, calls=%fused_computation.13.clone | custom fusion | bytes 4195328 | tf_op jit(solution)/shard_map/jit(_take)/gather | solution.py:203
  50.9 5.8 %gather_fusion.8 = f32[256,2048]{1,0:T(8,128)} fusion(f32[2048,512]{0,1:T(8,128)} %constant_dynamic-update-slice_fusion, s32[1024]{0:T(1024)S(1)} %get-tuple-element.84), kind=kCustom, calls=%fused_computation.12.clone | custom fusion | bytes 4195328 | tf_op jit(solution)/shard_map/jit(_take)/gather | solution.py:203
  56.7 5.8 %gather_fusion.7 = f32[256,2048]{1,0:T(8,128)} fusion(f32[2048,512]{0,1:T(8,128)} %constant_dynamic-update-slice_fusion, s32[1024]{0:T(1024)S(1)} %get-tuple-element.85), kind=kCustom, calls=%fused_computation.11.clone | custom fusion | bytes 4195328 | tf_op jit(solution)/shard_map/jit(_take)/gather | solution.py:203
  62.5 5.8 %gather_fusion.6 = f32[256,2048]{1,0:T(8,128)} fusion(f32[2048,512]{0,1:T(8,128)} %constant_dynamic-update-slice_fusion, s32[1024]{0:T(1024)S(1)} %get-tuple-element.86), kind=kCustom, calls=%fused_computation.10.clone | custom fusion | bytes 4195328 | tf_op jit(solution)/shard_map/jit(_take)/gather | solution.py:203
  68.4 5.8 %gather_fusion.5 = f32[256,2048]{1,0:T(8,128)} fusion(f32[2048,512]{0,1:T(8,128)} %constant_dynamic-update-slice_fusion, s32[1024]{0:T(1024)S(1)} %get-tuple-element.87), kind=kCustom, calls=%fused_computation.9.clone | custom fusion | bytes 4195328 | tf_op jit(solution)/shard_map/jit(_take)/gather | solution.py:203
  74.1 5.8 %gather_fusion.4 = f32[256,2048]{1,0:T(8,128)} fusion(f32[2048,512]{0,1:T(8,128)} %constant_dynamic-update-slice_fusion, s32[1024]{0:T(1024)S(1)} %get-tuple-element.88), kind=kCustom, calls=%fused_computation.1.clone | custom fusion | bytes 4195328 | tf_op jit(solution)/shard_map/jit(_take)/gather | solution.py:203
  79.9 22.3 %constant_dynamic-update-slice_fusion.9 = (f32[2048,512]{0,1:T(8,128)}, f32[2048,256]{0,1:T(8,128)S(1)}) fusion(f32[2048,256]{0,1:T(8,128)} %copy-done, f32[256]{0:T(256)S(1)} %bitcast.233, f32[256]{0:T(256)S(1)} %bitcast.257, f32[256]{0:T(256)S(1)} %bitcast.258, f32[256]{0:T(256)S(1)} %bitcast.256, f32[256]{0:T(256)S(1)} %bitcast.263, ...), kind=kLoop, calls=%fused_computation.163 | loop fusion | flops 33030144 | bytes 19016448
  102.2 1.7 fusion.84
  103.9 1.6 gather_fusion.13
  105.5 1.5 gather_fusion.12
  108.6 5.0 %psum.30 = f32[5,256]{1,0:T(8,128)S(1)} all-reduce(f32[5,256]{1,0:T(8,128)S(1)} %fusion.84), channel_id=1, replica_groups=mesh['vel'=2,'cell'=16] {'vel'}, use_global_device_ids=true, to_apply=%region_5.8 | all-reduce | flops 1280 | bytes 10240 | tf_op jit(solution)/shard_map/psum | solution.py:120
  113.6 1.9 select_bitcast_fusion
  115.5 1.9 select_bitcast_fusion.1
  117.5 0.9 select_bitcast_fusion.2
  118.4 0.9 select_bitcast_fusion.3
  119.3 8.9 %collective-permute-start.4 = (f32[2048,64]{0,1:T(8,128)}, f32[2048,64]{0,1:T(8,128)}, u32[]{:S(2)}, u32[]{:S(2)}) collective-permute-start(f32[2048,64]{0,1:T(8,128)} %select_bitcast_fusion.3), channel_id=1, source_target_pairs={{0,2},{1,3},{2,4},{3,5},{4,6},{5,7},{6,8},{7,9},{8,10},{9,11},{10,... | collective-permute-start | bytes 1572872 | tf_op jit(solution)/shard_map/ppermute | solution.py:22
  128.1 1.3 collective-permute-start.5
  129.4 1.3 collective-permute-start.6
  130.8 1.5 fusion.25
  132.3 4.9 %psum.31 = f32[3,256]{1,0:T(4,128)S(1)} all-reduce(f32[3,256]{1,0:T(4,128)S(1)} %pad_maximum_fusion.1), channel_id=1, replica_groups=mesh['vel'=2,'cell'=16] {'vel'}, use_global_device_ids=true, to_apply=%region_9.12 | all-reduce | flops 768 | bytes 6144 | tf_op jit(solution)/shard_map/psum | solution.py:148
  137.2 1.3 collective-permute-start.7
  138.5 18.3 %collective-permute-done.4 = f32[2048,64]{0,1:T(8,128)} collective-permute-done((f32[2048,64]{0,1:T(8,128)}, f32[2048,64]{0,1:T(8,128)}, u32[]{:S(2)}, u32[]{:S(2)}) %collective-permute-start.4) | collective-permute-done | bytes 524320 | tf_op jit(solution)/shard_map/ppermute | solution.py:22
  156.8 1.9 constant_dynamic-update-slice_fusion.8
  159.5 0.8 constant_dynamic-update-slice_fusion.6
  161.2 5.8 %gather_fusion.19 = f32[256,2048]{1,0:T(8,128)} fusion(f32[2048,512]{0,1:T(8,128)} %constant_dynamic-update-slice_fusion.5, s32[1024]{0:T(1024)S(1)} %get-tuple-element.83), kind=kCustom, calls=%fused_computation.19.clone | custom fusion | bytes 4195328 | tf_op jit(solution)/shard_map/jit(_take)/gather | solution.py:203
  167.0 5.8 %gather_fusion.18 = f32[256,2048]{1,0:T(8,128)} fusion(f32[2048,512]{0,1:T(8,128)} %constant_dynamic-update-slice_fusion.5, s32[1024]{0:T(1024)S(1)} %get-tuple-element.84), kind=kCustom, calls=%fused_computation.18.clone | custom fusion | bytes 4195328 | tf_op jit(solution)/shard_map/jit(_take)/gather | solution.py:203
  172.8 5.8 %gather_fusion.17 = f32[256,2048]{1,0:T(8,128)} fusion(f32[2048,512]{0,1:T(8,128)} %constant_dynamic-update-slice_fusion.5, s32[1024]{0:T(1024)S(1)} %get-tuple-element.85), kind=kCustom, calls=%fused_computation.17.clone | custom fusion | bytes 4195328 | tf_op jit(solution)/shard_map/jit(_take)/gather | solution.py:203
  178.6 5.8 %gather_fusion.16 = f32[256,2048]{1,0:T(8,128)} fusion(f32[2048,512]{0,1:T(8,128)} %constant_dynamic-update-slice_fusion.5, s32[1024]{0:T(1024)S(1)} %get-tuple-element.86), kind=kCustom, calls=%fused_computation.16.clone | custom fusion | bytes 4195328 | tf_op jit(solution)/shard_map/jit(_take)/gather | solution.py:203
  184.4 5.8 %gather_fusion.15 = f32[256,2048]{1,0:T(8,128)} fusion(f32[2048,512]{0,1:T(8,128)} %constant_dynamic-update-slice_fusion.5, s32[1024]{0:T(1024)S(1)} %get-tuple-element.87), kind=kCustom, calls=%fused_computation.15.clone | custom fusion | bytes 4195328 | tf_op jit(solution)/shard_map/jit(_take)/gather | solution.py:203
  190.2 5.8 %gather_fusion.14 = f32[256,2048]{1,0:T(8,128)} fusion(f32[2048,512]{0,1:T(8,128)} %constant_dynamic-update-slice_fusion.5, s32[1024]{0:T(1024)S(1)} %get-tuple-element.88), kind=kCustom, calls=%fused_computation.14.clone | custom fusion | bytes 4195328 | tf_op jit(solution)/shard_map/jit(_take)/gather | solution.py:203
  196.0 9.2 %fusion.35 = f32[2048,256]{0,1:T(8,128)} fusion(f32[2048,256]{0,1:T(8,128)S(1)} %get-tuple-element.19, f32[256,2048]{1,0:T(8,128)} %gather_fusion.19, f32[256,2048]{1,0:T(8,128)} %gather_fusion.18, f32[256,2048]{1,0:T(8,128)} %gather_fusion.17, f32[256,2048]{1,0:T(8,128)} %gather_fusion.16, f32[256,2048]{1,0:T(8,128)} %gather_fusion.15, ...), kind=kLoop, calls=%fused_computation.73 | loop fusion | flops 33030144 | bytes 16919296 | tf_op jit(solution)/shard_map/jit(_where)/select_n | solution.py:212
  205.2 2.9 %copy.36 = f32[2048,256]{1,0:T(8,128)} copy(f32[2048,256]{0,1:T(8,128)} %fusion.35) | data formatting | bytes 4194304 | tf_op jit(solution)/shard_map/jit(_where)/select_n | solution.py:212
  (67 shorter events, 10.3 us)
Async XLA Ops:
  2.8 26.8 %copy-start = (f32[2048,256]{0,1:T(8,128)}, f32[2048,256]{0,1:T(8,128)S(1)}, u32[]{:S(2)}) copy-start(f32[2048,256]{0,1:T(8,128)S(1)} %copy.33) | copy-start | bytes 6291460
  4.5 39.8 %collective-permute-start.3 = (f32[2048,64]{0,1:T(8,128)}, f32[2048,64]{0,1:T(8,128)S(1)}, u32[]{:S(2)}, u32[]{:S(2)}) collective-permute-start(f32[2048,64]{0,1:T(8,128)} %select_bitcast_fusion.4), channel_id=1, source_target_pairs={{2,0},{3,1},{4,2},{5,3},{6,4},{7,5},{8,6},{9,7},{10,8},{11,9},{12,... | collective-permute-start | bytes 1572872 | tf_op jit(solution)/shard_map/ppermute | solution.py:22
  7.4 31.2 %collective-permute-start = (f32[2048,64]{0,1:T(8,128)}, f32[2048,64]{0,1:T(8,128)}, u32[]{:S(2)}, u32[]{:S(2)}) collective-permute-start(f32[2048,64]{0,1:T(8,128)} %select_bitcast_fusion.7), channel_id=1, source_target_pairs={{0,2},{1,3},{2,4},{3,5},{4,6},{5,7},{6,8},{7,9},{8,10},{9,11},{10,... | collective-permute-start | bytes 1572872 | tf_op jit(solution)/shard_map/ppermute | solution.py:22
  15.4 25.1 %collective-permute-start.1 = (f32[2048,64]{0,1:T(8,128)}, f32[2048,64]{0,1:T(8,128)}, u32[]{:S(2)}, u32[]{:S(2)}) collective-permute-start(f32[2048,64]{0,1:T(8,128)} %select_bitcast_fusion.6), channel_id=1, source_target_pairs={{0,1},{1,2},{2,3},{3,4},{4,5},{5,6},{6,7},{7,8},{8,9},{9,10},{10,1... | collective-permute-start | bytes 1572872 | tf_op jit(solution)/shard_map/ppermute | solution.py:22
  17.6 3.0 %copy-start.2 = (s32[6,256]{1,0:T(8,128)S(1)}, s32[6,256]{1,0:T(8,128)}, u32[]{:S(2)}) copy-start(s32[6,256]{1,0:T(8,128)} %param.14) | copy-start | bytes 18436
  17.6 4.2 %copy-start.3 = (s32[256]{0:T(256)S(1)}, s32[256]{0:T(256)}, u32[]{:S(2)}) copy-start(s32[256]{0:T(256)} %param.12) | copy-start | bytes 3076
  17.7 4.3 %copy-start.1 = (s32[6,256]{1,0:T(8,128)S(1)}, s32[6,256]{1,0:T(8,128)}, u32[]{:S(2)}) copy-start(s32[6,256]{1,0:T(8,128)} %param.15) | copy-start | bytes 18436
  19.4 23.0 %collective-permute-start.2 = (f32[2048,64]{0,1:T(8,128)}, f32[2048,64]{0,1:T(8,128)}, u32[]{:S(2)}, u32[]{:S(2)}) collective-permute-start(f32[2048,64]{0,1:T(8,128)} %select_bitcast_fusion.5), channel_id=1, source_target_pairs={{1,0},{2,1},{3,2},{4,3},{5,4},{6,5},{7,6},{8,7},{9,8},{10,9},{11,1... | collective-permute-start | bytes 1572872 | tf_op jit(solution)/shard_map/ppermute | solution.py:22
  119.3 37.6 %collective-permute-start.4 = (f32[2048,64]{0,1:T(8,128)}, f32[2048,64]{0,1:T(8,128)}, u32[]{:S(2)}, u32[]{:S(2)}) collective-permute-start(f32[2048,64]{0,1:T(8,128)} %select_bitcast_fusion.3), channel_id=1, source_target_pairs={{0,2},{1,3},{2,4},{3,5},{4,6},{5,7},{6,8},{7,9},{8,10},{9,11},{10,... | collective-permute-start | bytes 1572872 | tf_op jit(solution)/shard_map/ppermute | solution.py:22
  128.1 30.6 %collective-permute-start.5 = (f32[2048,64]{0,1:T(8,128)}, f32[2048,64]{0,1:T(8,128)S(1)}, u32[]{:S(2)}, u32[]{:S(2)}) collective-permute-start(f32[2048,64]{0,1:T(8,128)} %select_bitcast_fusion.2), channel_id=1, source_target_pairs={{0,1},{1,2},{2,3},{3,4},{4,5},{5,6},{6,7},{7,8},{8,9},{9,10},{10,1... | collective-permute-start | bytes 1572872 | tf_op jit(solution)/shard_map/ppermute | solution.py:22
  129.4 30.1 %collective-permute-start.6 = (f32[2048,64]{0,1:T(8,128)}, f32[2048,64]{0,1:T(8,128)S(1)}, u32[]{:S(2)}, u32[]{:S(2)}) collective-permute-start(f32[2048,64]{0,1:T(8,128)} %select_bitcast_fusion.1), channel_id=1, source_target_pairs={{1,0},{2,1},{3,2},{4,3},{5,4},{6,5},{7,6},{8,7},{9,8},{10,9},{11,1... | collective-permute-start | bytes 1572872 | tf_op jit(solution)/shard_map/ppermute | solution.py:22
  137.2 23.1 %collective-permute-start.7 = (f32[2048,64]{0,1:T(8,128)}, f32[2048,64]{0,1:T(8,128)S(1)}, u32[]{:S(2)}, u32[]{:S(2)}) collective-permute-start(f32[2048,64]{0,1:T(8,128)} %select_bitcast_fusion), channel_id=1, source_target_pairs={{2,0},{3,1},{4,2},{5,3},{6,4},{7,5},{8,6},{9,7},{10,8},{11,9},{12,... | collective-permute-start | bytes 1572872 | tf_op jit(solution)/shard_map/ppermute | solution.py:22
where the time goes:
time: 207 us; the launch traced here: 208 us
  local copies, waits for them, and re-layouts  93 us (45%)
  other arithmetic  46.7 us (23%)
  starting transfers between devices  23.8 us (11%)
  blocking collectives  20.1 us (10%)
  waiting for transfers between devices  19.1 us (9%)
  matrix products  4.24 us (2%)
    gather x12, local copies, waits for them, and re-layouts, advance(): across = jnp.take(extended, face_neighbour[face_slot], axis=1)  69.6 us
    unnamed x2, other arithmetic  24.4 us
    ppermute x8, starting transfers between devices, from_behind(): return lax.ppermute(block, axis, route)  23.8 us
    ppermute x8, waiting for transfers between devices, from_behind(): return lax.ppermute(block, axis, route)  19.1 us
    unnamed x15, local copies, waits for them, and re-layouts  11.2 us
    psum x2, blocking collectives, integral_entries(): summed = lax.psum(partial_heat, 'vel')  10.1 us
    psum x2, blocking collectives, integral_entries(): lax.psum(jnp.dot(matrix, state_values, precision=lax.Precision.HIGHEST),...  10 us
    select_n x8, other arithmetic, ghost_columns(): packet = jnp.take(state_values, send_list[3 - group_id], axis=1)  9.36 us
  transfers between devices with their start and end apart: 8, of which 2 were waited for; matrix products, arithmetic and copies ran while one was open for 11% of the time, Pallas kernels for 0%

commit v1 on v0

v1 whole, which is shorter than its diff:
```python
import functools
import math

import jax
import jax.numpy as jnp
from jax import lax
from jax.experimental import pallas as pl
from jax.experimental.pallas import tpu as pltpu
from jax.sharding import PartitionSpec as P

NV = 16
STEPS = 2
SPEED_LIMIT = 5.0
SPACING = 2.0 * SPEED_LIMIT / NV
DT = 0.03
DRAG = 0.5
POWER = 0.81
PRANDTL_TERM = 1.0 - 2.0 / 3.0
WEIGHT = SPACING**3 * (2.0 * math.pi) ** (-1.5)
OFFSETS = (-2, -1, 1, 2)
F32 = jnp.float32
BF16 = jnp.bfloat16


def node(index):
    return -SPEED_LIMIT + (index + 0.5) * SPACING


def split(values):
    high = values.astype(BF16)
    return high, (values - high.astype(F32)).astype(BF16)


def kernel(
    n_cell, n_vel, planes,
    dist, count, level, sends, faces, face_level, out,
    state1, send_buf, recv_buf, pick, move, acc, part, parts, b_terms, e_terms, c_terms, ratios,
    send_sem, recv_sem, part_send, part_recv,
):
    d = lax.axis_index("cell")
    vel = lax.axis_index("vel")
    first_a = vel * planes
    there = [jnp.logical_and(d + o >= 0, d + o < n_cell) for o in OFFSETS]
    live = lax.broadcasted_iota(jnp.int32, (8, 256), 1) < count[0]
    low_lanes = lax.broadcasted_iota(jnp.int32, (128, 128), 1) < 64

    barrier = pltpu.get_barrier_semaphore()
    for j, o in enumerate(OFFSETS):
        @pl.when(there[j])
        def _(o=o):
            pl.semaphore_signal(barrier, inc=1, device_id={"cell": d + o})
    for k in range(1, n_vel):
        pl.semaphore_signal(barrier, inc=1, device_id={"vel": lax.rem(vel + k, n_vel)})

    cells = lax.broadcasted_iota(jnp.int32, (256, 256), 0)
    pick[...] = jnp.where(cells == sends[...], 1.0, 0.0).astype(BF16)
    own = level[...]
    ratio = jnp.exp2((3 * own - 2 * jnp.maximum(own, face_level[...])).astype(F32))
    columns = lax.broadcasted_iota(jnp.int32, (512, 256), 0)
    west = first_a < NV // 2
    in_x = jnp.where(west, faces[0:1], faces[1:2])
    ratio_in = jnp.where(west, ratio[0:1], ratio[1:2])
    ratio_out = jnp.where(west, ratio[1:2], ratio[0:1])
    move[0] = jnp.where(columns == in_x, ratio_in, 0.0).astype(BF16)
    for k in range(2, 6):
        move[k - 1] = jnp.where(columns == faces[k:k + 1], ratio[k:k + 1], 0.0).astype(BF16)
        ratios[k] = jnp.broadcast_to(ratio[k:k + 1], (8, 256))
    ratios[0] = jnp.broadcast_to(ratio_out, (8, 256))

    pl.semaphore_wait(barrier, n_vel - 1 + sum(t.astype(jnp.int32) for t in there))
    for j in range(4):
        @pl.when(jnp.logical_not(there[j]))
        def _(j=j):
            for s in range(STEPS):
                def clear(p, carry):
                    recv_buf[s, p, j] = jnp.zeros((128, 128), F32)
                    return carry
                lax.fori_loop(0, planes, clear, 0)

    def message(s, p, j):
        return pltpu.make_async_remote_copy(
            src_ref=send_buf.at[s, p, j],
            dst_ref=recv_buf.at[s, p, 3 - j],
            send_sem=send_sem.at[s, p, j],
            recv_sem=recv_sem.at[s, p, 3 - j],
            device_id={"cell": d + OFFSETS[j]},
        )

    def send_plane(s, p, high, low):
        both = jnp.dot(jnp.concatenate([high, low], 0), pick[...], preferred_element_type=F32)
        packed = both[:256] + both[256:]
        for pair in range(2):
            upper = packed[:128, pair * 128:pair * 128 + 128]
            lower = packed[128:, pair * 128:pair * 128 + 128]
            send_buf[s, p, 2 * pair] = jnp.where(low_lanes, upper, pltpu.roll(lower, 64, 1))
            send_buf[s, p, 2 * pair + 1] = jnp.where(low_lanes, pltpu.roll(upper, 64, 1), lower)
        for j in range(4):
            @pl.when(there[j])
            def _(j=j):
                message(s, p, j).start()

    def add_moments(p, plane):
        c = node((first_a + p).astype(F32))
        acc[0] += plane
        acc[1] += c * plane
        acc[2] += (c * c) * plane
        acc[3] += (c * c * c) * plane

    def finish_moments(s):
        nodes = [node(lax.broadcasted_iota(jnp.int32, (8, 256), 0).astype(F32) + 8.0 * eh) for eh in range(2)]
        u = {}
        for q in range(4):
            for r in range(4 - q):
                for eh in range(2):
                    total = None
                    for b in range(NV):
                        row = acc[q, pl.ds(eh * 128 + b * 8, 8), :]
                        term = row if r == 0 else row * (node(b) ** r)
                        total = term if total is None else total + term
                    u[q, r, eh] = total

        def moment(q, r, t):
            value = 0.0
            for eh in range(2):
                term = u[q, r, eh]
                for _ in range(t):
                    term = term * nodes[eh]
                value = value + term
            return value

        rows = [
            moment(0, 0, 0), moment(1, 0, 0), moment(0, 1, 0), moment(0, 0, 1),
            moment(2, 0, 0), moment(0, 2, 0), moment(0, 0, 2),
            moment(1, 1, 0), moment(1, 0, 1), moment(0, 1, 1),
            moment(3, 0, 0) + moment(1, 2, 0) + moment(1, 0, 2),
            moment(2, 1, 0) + moment(0, 3, 0) + moment(0, 1, 2),
            moment(2, 0, 1) + moment(0, 2, 1) + moment(0, 0, 3),
        ]
        for i, value in enumerate(rows):
            part[s, i:i + 1] = WEIGHT * jnp.sum(value, 0, keepdims=True)
        part[s, 13:16] = jnp.zeros((3, 256), F32)
        copies = []
        for k in range(1, n_vel):
            copies.append(pltpu.make_async_remote_copy(
                src_ref=part.at[s], dst_ref=parts.at[s, k],
                send_sem=part_send.at[s, k], recv_sem=part_recv.at[s, k],
                device_id={"vel": lax.rem(vel + k, n_vel)},
            ))
        for copy in copies:
            copy.start()
        for copy in copies:
            copy.wait()
        total = part[s]
        for k in range(1, n_vel):
            total = total + parts[s, k]
        m = [jnp.broadcast_to(total[i:i + 1], (8, 256)) for i in range(13)]
        density = m[0]
        safe = jnp.where(live, density, 1.0)
        mean = [m[i] / safe for i in (1, 2, 3)]
        energy = m[4] + m[5] + m[6]
        speed = mean[0] * mean[0] + mean[1] * mean[1] + mean[2] * mean[2]
        temperature = jnp.where(live, (energy / safe - speed) / 3.0, 1.0)
        second = ((m[4], m[7], m[8]), (m[7], m[5], m[9]), (m[8], m[9], m[6]))
        along = mean[0] * m[1] + mean[1] * m[2] + mean[2] * m[3]
        heat = []
        for i in range(3):
            cross = sum(mean[k] * second[i][k] for k in range(3))
            heat.append(0.5 * (
                m[10 + i] - 2.0 * cross + speed * m[1 + i]
                - mean[i] * (energy - 2.0 * along + speed * density)
            ))
        pressure = safe * temperature
        log_t = jnp.log(temperature)
        rate = pressure / (DRAG * jnp.exp(POWER * log_t))
        inverse = 1.0 / temperature
        factor = PRANDTL_TERM / (5.0 * pressure * temperature)
        c_terms[0] = mean[0]
        c_terms[1] = inverse
        c_terms[2] = factor * heat[0]
        c_terms[3] = DT * rate * density * jnp.exp(-1.5 * log_t)
        c_terms[4] = 1.0 - DT * rate
        for b in range(NV):
            c = node(b)
            width = c - mean[1]
            square = width * width * inverse
            at = pl.ds(b * 8, 8)
            b_terms[0, at, :] = jnp.exp(-0.5 * square)
            b_terms[1, at, :] = factor * heat[1] * width
            b_terms[2, at, :] = square
            b_terms[3, at, :] = (DT * abs(c)) * ratios[3 if c < 0 else 2]
        for eh in range(2):
            width = nodes[eh] - mean[2]
            square = width * width * inverse
            e_terms[0, eh] = jnp.exp(-0.5 * square)
            e_terms[1, eh] = factor * heat[2] * width
            e_terms[2, eh] = square - 5.0
            e_terms[3, eh] = (DT * jnp.abs(nodes[eh])) * ratios[5 if eh == 0 else 4]

    def advance_plane(s, p, plane):
        for g in range(4):
            @pl.when(there[g])
            def _(g=g):
                pltpu.make_async_remote_copy(
                    src_ref=send_buf.at[s, p, g], dst_ref=recv_buf.at[s, p, g],
                    send_sem=send_sem.at[s, p, g], recv_sem=recv_sem.at[s, p, g],
                    device_id={"cell": d + OFFSETS[g]},
                ).wait_recv()
        pieces = [plane]
        for pair in range(2):
            first, second = recv_buf[s, p, 2 * pair], recv_buf[s, p, 2 * pair + 1]
            pieces.append(jnp.concatenate([
                jnp.where(low_lanes, first, pltpu.roll(second, 64, 1)),
                jnp.where(low_lanes, pltpu.roll(first, 64, 1), second),
            ], 0))
        high, low = split(jnp.concatenate(pieces, 1))

        def across(k, spans):
            left = jnp.concatenate([h[i:j] for h in (high, low) for i, j in spans], 0)
            both = jnp.dot(left, move[k], preferred_element_type=F32)
            half = both.shape[0] // 2
            return both[:half] + both[half:]

        xs = across(0, [(0, 256)])
        ys = [across(1, [(0, 64), (128, 192)]), across(2, [(64, 128), (192, 256)])]
        zs = [across(3, [(0, 128)]), across(4, [(128, 256)])]
        c = node((first_a + p).astype(F32))
        speed = DT * jnp.abs(c)
        width = c - c_terms[0]
        square = width * width * c_terms[1]
        a_gauss = c_terms[3] * jnp.exp(-0.5 * square)
        a_heat = c_terms[2] * width
        a_keep = c_terms[4] - speed * ratios[0]
        rows = []
        for eh in range(2):
            e_node = node(lax.broadcasted_iota(jnp.int32, (8, 256), 0).astype(F32) + 8.0 * eh)
            e_speed = DT * jnp.abs(e_node)
            gauss = a_gauss * e_terms[0, eh]
            warm = a_heat + e_terms[1, eh]
            shape = square + e_terms[2, eh]
            keep = a_keep - e_terms[3, eh]
            for b in range(NV):
                at = eh * 128 + b * 8
                bs = pl.ds(b * 8, 8)
                iy = (b % 8) * 8 + 64 * eh
                f = plane[at:at + 8]
                shakhov = gauss * b_terms[0, bs, :] * (
                    1.0 + (warm + b_terms[1, bs, :]) * (shape + b_terms[2, bs, :])
                )
                new = f * (keep - b_terms[3, bs, :]) + shakhov
                new = new + speed * xs[at:at + 8]
                new = new + (DT * abs(node(b))) * ys[b // 8][iy:iy + 8]
                new = new + e_speed * zs[eh][b * 8:b * 8 + 8]
                rows.append(jnp.where(live, new, 0.0))
        return jnp.concatenate(rows, 0)

    def load_plane(p):
        return jnp.concatenate([dist[p, :, eh].reshape(128, 256) for eh in range(2)], 0)

    def first_send(p, carry):
        high, low = split(load_plane(p))
        send_plane(0, p, high, low)
        return carry

    lax.fori_loop(0, planes, first_send, 0)
    acc[...] = jnp.zeros_like(acc)

    def first_moments(p, carry):
        add_moments(p, load_plane(p))
        return carry

    lax.fori_loop(0, planes, first_moments, 0)
    finish_moments(0)
    acc[...] = jnp.zeros_like(acc)

    def first_step(p, carry):
        new = advance_plane(0, p, load_plane(p))
        high, low = split(new)
        send_plane(1, p, high, low)
        state1[p] = new
        add_moments(p, new)
        return carry

    lax.fori_loop(0, planes, first_step, 0)
    finish_moments(1)

    def second_step(p, carry):
        new = advance_plane(1, p, state1[p])
        for eh in range(2):
            out[p, :, eh] = new[eh * 128:eh * 128 + 128].reshape(16, 8, 256)
        return carry

    lax.fori_loop(0, planes, second_step, 0)

    def drain(p, carry):
        for s in range(STEPS):
            for j in range(4):
                @pl.when(there[j])
                def _(s=s, j=j):
                    message(s, p, j).wait_send()
        return carry

    lax.fori_loop(0, planes, drain, 0)


def solution(mesh):
    n_cell, n_vel = mesh.shape["cell"], mesh.shape["vel"]

    def body(distribution, cell_count, cell_level, send_list, face_neighbour, face_level):
        rows, width = distribution.shape
        planes = rows // (NV * NV)
        shape = (planes, NV, 2, NV // 2, width)
        vmem = pl.BlockSpec(memory_space=pltpu.VMEM)
        result = pl.pallas_call(
            functools.partial(kernel, n_cell, n_vel, planes),
            out_shape=jax.ShapeDtypeStruct(shape, F32),
            in_specs=[vmem, pl.BlockSpec(memory_space=pltpu.SMEM), vmem, vmem, vmem, vmem],
            out_specs=vmem,
            scratch_shapes=[
                pltpu.VMEM((planes, 256, 256), F32),
                pltpu.VMEM((STEPS, planes, 4, 128, 128), F32),
                pltpu.VMEM((STEPS, planes, 4, 128, 128), F32),
                pltpu.VMEM((256, 256), BF16),
                pltpu.VMEM((5, 512, 256), BF16),
                pltpu.VMEM((4, 256, 256), F32),
                pltpu.VMEM((STEPS, 16, 256), F32),
                pltpu.VMEM((STEPS, n_vel, 16, 256), F32),
                pltpu.VMEM((4, 128, 256), F32),
                pltpu.VMEM((4, 2, 8, 256), F32),
                pltpu.VMEM((5, 8, 256), F32),
                pltpu.VMEM((6, 8, 256), F32),
                pltpu.SemaphoreType.DMA((STEPS, planes, 4)),
                pltpu.SemaphoreType.DMA((STEPS, planes, 4)),
                pltpu.SemaphoreType.DMA((STEPS, n_vel)),
                pltpu.SemaphoreType.DMA((STEPS, n_vel)),
            ],
            compiler_params=pltpu.CompilerParams(
                collective_id=0, has_side_effects=True, vmem_limit_bytes=48 * 2**20
            ),
        )(
            distribution.reshape(shape),
            cell_count,
            cell_level.reshape(1, width),
            send_list.reshape(1, width),
            face_neighbour,
            face_level,
        )
        return result.reshape(rows, width)

    placed = (P("vel", "cell"), P("cell"), P("cell"), P(None, "cell"), P(None, "cell"), P(None, "cell"))
    return jax.shard_map(body, mesh=mesh, in_specs=placed, out_specs=P("vel", "cell"), check_vma=False)
```

time: 207 us -> 80.3 us (0.39)
  the two profiles are of different devices: /device:TPU:0 before, /device:TPU:13 now
where the time goes in v1:
time: 80.3 us; the launch traced here: 80 us
  Pallas kernels  73.6 us (92%)
  local copies, waits for them, and re-layouts  5.75 us (7%)
    pallas_call x1, Pallas kernels, body(): pl.pallas_call(functools.partial(kernel, n_cell, n_vel, planes), out_shap...  73.6 us
    unnamed x9, local copies, waits for them, and re-layouts  4.98 us

profile of v1, /device:TPU:13, one launch (start us, length us, event | category | flops | bytes accessed | tf_op | source)
XLA Modules:
  0.0 80.0 jit_solution(5898395413531399896)
XLA Ops:
  0.7 0.8 reshape.14.sends
  1.4 0.0 copy-start
  1.4 1.6 %copy-done = f32[2048,256]{1,0:T(8,128)S(1)} copy-done((f32[2048,256]{1,0:T(8,128)S(1)}, f32[2048,256]{1,0:T(8,128)}, u32[]{:S(2)}) %copy-start) | copy-done | bytes 2097176
  3.0 0.0 copy-start.1
  3.0 0.7 copy-done.1
  3.7 0.0 copy-start.2
  3.7 0.7 copy-done.2
  4.4 0.0 copy-start.3
  4.4 0.7 copy-done.3
  5.1 73.6 %shard_map.64 = f32[8,16,2,8,256]{4,3,2,1,0:T(8,128)S(1)} custom-call(f32[8,16,2,8,256]{4,3,2,1,0:T(8,128)S(1)} %bitcast.4, s32[1]{0:T(128)S(6)} %copy.8.count, s32[1,256]{1,0:T(1,128)S(1)} %bitcast.5, s32[1,256]{1,0:T(1,128)S(1)} %reshape.14.sends, s32[6,256]{1,0:T(8,128)S(1)} %copy-done.1, s32[6,256]{1,0:T(8,128)S(1)} %copy-done.2), custom_call_target="tpu_custom_call" | custom-call | tf_op jit(solution)/shard_map/pallas_call | solution.py:313
  78.6 1.3 %copy.9 = f32[2048,256]{1,0:T(8,128)} copy(f32[2048,256]{1,0:T(8,128)S(1)} %bitcast.3) | data formatting | bytes 4194304
Async XLA Ops:
  1.4 1.6 %copy-start = (f32[2048,256]{1,0:T(8,128)S(1)}, f32[2048,256]{1,0:T(8,128)}, u32[]{:S(2)}) copy-start(f32[2048,256]{1,0:T(8,128)} %param.6) | copy-start | bytes 6291460
  3.0 0.7 copy-start.1
  3.7 0.7 copy-start.2
  4.4 0.7 copy-start.3

commit v2 on v1

v2 whole, which is shorter than its diff:
```python
import functools
import math

import jax
import jax.numpy as jnp
from jax import lax
from jax.experimental import pallas as pl
from jax.experimental.pallas import tpu as pltpu
from jax.sharding import PartitionSpec as P

NV = 16
STEPS = 2
SPEED_LIMIT = 5.0
SPACING = 2.0 * SPEED_LIMIT / NV
DT = 0.03
DRAG = 0.5
POWER = 0.81
PRANDTL_TERM = 1.0 - 2.0 / 3.0
WEIGHT = SPACING**3 * (2.0 * math.pi) ** (-1.5)
OFFSETS = (-2, -1, 1, 2)
F32 = jnp.float32
BF16 = jnp.bfloat16


def node(index):
    return -SPEED_LIMIT + (index + 0.5) * SPACING


def split(values):
    high = values.astype(BF16)
    return high, (values - high.astype(F32)).astype(BF16)


def kernel(
    n_cell, n_vel, planes,
    dist, meta_in, out,
    meta, bulk, out_buf, state1, send_buf, recv_buf, pick, move, acc, part, parts,
    b_terms, e_terms, c_terms, ratios,
    send_sem, recv_sem, part_send, part_recv, bulk_send, bulk_recv, out_send, out_recv, meta_send, meta_recv,
):
    half = planes // 2
    d = lax.axis_index("cell")
    vel = lax.axis_index("vel")
    group = d // 4
    x = (d // 2) % 2
    core = d % 2
    other = 1 - x
    partner = d + 2 - 4 * x
    base = vel * planes
    first_a = base + x * half
    low_lanes = lax.broadcasted_iota(jnp.int32, (128, 128), 1) < 64
    below = group > 0
    above = group < n_cell // 4 - 1

    barrier = pltpu.get_barrier_semaphore()
    pl.semaphore_signal(barrier, inc=1, device_id={"cell": d + 1 - 2 * core})

    @pl.when(below)
    def _():
        pl.semaphore_signal(barrier, inc=1, device_id={"cell": d - 4})

    @pl.when(jnp.logical_and(below, core == 0))
    def _():
        pl.semaphore_signal(barrier, inc=1, device_id={"cell": d - 3})

    @pl.when(above)
    def _():
        pl.semaphore_signal(barrier, inc=1, device_id={"cell": d + 4})

    @pl.when(jnp.logical_and(above, core == 1))
    def _():
        pl.semaphore_signal(barrier, inc=1, device_id={"cell": d + 3})

    def peer(k):
        return {"cell": d if k < n_vel else partner, "vel": lax.rem(vel + k % n_vel, n_vel)}

    for k in range(1, 2 * n_vel):
        pl.semaphore_signal(barrier, inc=1, device_id=peer(k))
    is_below, is_above = below.astype(jnp.int32), above.astype(jnp.int32)
    pl.semaphore_wait(barrier, 2 * n_vel + is_below * (2 - core) + is_above * (1 + core))

    meta_copy = pltpu.make_async_remote_copy(
        src_ref=meta_in, dst_ref=meta.at[x], send_sem=meta_send, recv_sem=meta_recv,
        device_id={"cell": partner},
    )
    meta_copy.start()

    def bulk_copy(p):
        return pltpu.make_async_remote_copy(
            src_ref=dist.at[other * half + p], dst_ref=bulk.at[p],
            send_sem=bulk_send.at[p], recv_sem=bulk_recv.at[p], device_id={"cell": partner},
        )

    def out_copy(p):
        return pltpu.make_async_remote_copy(
            src_ref=out_buf.at[p], dst_ref=out.at[x * half + p],
            send_sem=out_send.at[p], recv_sem=out_recv.at[p], device_id={"cell": partner},
        )

    bulk_copy(0).start()

    def live_cells(t):
        return lax.broadcasted_iota(jnp.int32, (8, 256), 1) < meta[t, 14:15]

    def matrices(t):
        cells = lax.broadcasted_iota(jnp.int32, (256, 256), 0)
        pick[t] = jnp.where(cells == meta[t, 13:14], 1.0, 0.0).astype(BF16)
        own = meta[t, 12:13]
        ratio = jnp.exp2((3 * own - 2 * jnp.maximum(own, meta[t, 6:12])).astype(F32))
        faces = meta[t, 0:6]
        columns = lax.broadcasted_iota(jnp.int32, (512, 256), 0)
        west = base < NV // 2
        in_x = jnp.where(west, faces[0:1], faces[1:2])
        ratio_in = jnp.where(west, ratio[0:1], ratio[1:2])
        ratio_out = jnp.where(west, ratio[1:2], ratio[0:1])
        move[t, 0] = jnp.where(columns == in_x, ratio_in, 0.0).astype(BF16)
        for k in range(2, 6):
            move[t, k - 1] = jnp.where(columns == faces[k:k + 1], ratio[k:k + 1], 0.0).astype(BF16)
            ratios[t, k] = jnp.broadcast_to(ratio[k:k + 1], (8, 256))
        ratios[t, 0] = jnp.broadcast_to(ratio_out, (8, 256))

    def block(t, o):
        there = 4 * group + 2 * t + core + o
        inside = jnp.logical_and(there >= 0, there < n_cell)
        there = jnp.clip(there, 0, n_cell - 1)
        return inside, 4 * (there // 4) + 2 * x + there % 2, (there // 2) % 2

    def is_local(t, j):
        return {0: t == 1, 3: t == 0}.get(j)

    def remote(t, j):
        inside, _, _ = block(t, OFFSETS[j])
        local = is_local(t, j)
        return inside if local is None else jnp.logical_and(inside, jnp.logical_not(local))

    def message(s, t, p, j):
        _, device, place = block(t, OFFSETS[j])
        return pltpu.make_async_remote_copy(
            src_ref=send_buf.at[s, t, p, j],
            dst_ref=recv_buf.at[s, place, p, 3 - j],
            send_sem=send_sem.at[s, t, p, j],
            recv_sem=recv_sem.at[s, place, p, 3 - j],
            device_id={"cell": device},
        )

    def send_plane(s, t, p, plane):
        high, low = split(plane)
        both = jnp.dot(jnp.concatenate([high, low], 0), pick[t], preferred_element_type=F32)
        packed = both[:256] + both[256:]
        values = []
        for pair in range(2):
            upper = packed[:128, pair * 128:pair * 128 + 128]
            lower = packed[128:, pair * 128:pair * 128 + 128]
            values.append(jnp.where(low_lanes, upper, pltpu.roll(lower, 64, 1)))
            values.append(jnp.where(low_lanes, pltpu.roll(upper, 64, 1), lower))
        for j in range(4):
            @pl.when(remote(t, j))
            def _(j=j):
                send_buf[s, t, p, j] = values[j]
                message(s, t, p, j).start()
            if j in (0, 3):
                @pl.when(is_local(t, j))
                def _(j=j):
                    recv_buf[s, 1 - t, p, 3 - j] = values[j]

    def add_moments(t, a, plane):
        c = node(a.astype(F32))
        acc[t, 0] += plane
        acc[t, 1] += c * plane
        acc[t, 2] += (c * c) * plane
        acc[t, 3] += (c * c * c) * plane

    nodes = [node(lax.broadcasted_iota(jnp.int32, (8, 256), 0).astype(F32) + 8.0 * eh) for eh in range(2)]

    def reduce_moments(s, t):
        u = {}
        for q in range(4):
            for r in range(4 - q):
                for eh in range(2):
                    total = None
                    for b in range(NV):
                        row = acc[t, q, pl.ds(eh * 128 + b * 8, 8), :]
                        term = row if r == 0 else row * (node(b) ** r)
                        total = term if total is None else total + term
                    u[q, r, eh] = total

        def moment(q, r, e):
            value = 0.0
            for eh in range(2):
                term = u[q, r, eh]
                for _ in range(e):
                    term = term * nodes[eh]
                value = value + term
            return value

        rows = [
            moment(0, 0, 0), moment(1, 0, 0), moment(0, 1, 0), moment(0, 0, 1),
            moment(2, 0, 0), moment(0, 2, 0), moment(0, 0, 2),
            moment(1, 1, 0), moment(1, 0, 1), moment(0, 1, 1),
            moment(3, 0, 0) + moment(1, 2, 0) + moment(1, 0, 2),
            moment(2, 1, 0) + moment(0, 3, 0) + moment(0, 1, 2),
            moment(2, 0, 1) + moment(0, 2, 1) + moment(0, 0, 3),
        ]
        sums = [WEIGHT * jnp.sum(value, 0, keepdims=True) for value in rows]
        part[s, t] = jnp.concatenate(sums + [jnp.zeros((3, 256), F32)], 0)

    def part_copy(s, k):
        return pltpu.make_async_remote_copy(
            src_ref=part.at[s], dst_ref=parts.at[s, k],
            send_sem=part_send.at[s, k], recv_sem=part_recv.at[s, k], device_id=peer(k),
        )

    def terms(s, t):
        live = live_cells(t)
        total = part[s, t]
        for k in range(1, 2 * n_vel):
            total = total + parts[s, k, t]
        m = [jnp.broadcast_to(total[i:i + 1], (8, 256)) for i in range(13)]
        density = m[0]
        safe = jnp.where(live, density, 1.0)
        mean = [m[i] / safe for i in (1, 2, 3)]
        energy = m[4] + m[5] + m[6]
        speed = mean[0] * mean[0] + mean[1] * mean[1] + mean[2] * mean[2]
        temperature = jnp.where(live, (energy / safe - speed) / 3.0, 1.0)
        second = ((m[4], m[7], m[8]), (m[7], m[5], m[9]), (m[8], m[9], m[6]))
        along = mean[0] * m[1] + mean[1] * m[2] + mean[2] * m[3]
        heat = []
        for i in range(3):
            cross = sum(mean[k] * second[i][k] for k in range(3))
            heat.append(0.5 * (
                m[10 + i] - 2.0 * cross + speed * m[1 + i]
                - mean[i] * (energy - 2.0 * along + speed * density)
            ))
        pressure = safe * temperature
        log_t = jnp.log(temperature)
        rate = pressure / (DRAG * jnp.exp(POWER * log_t))
        inverse = 1.0 / temperature
        factor = PRANDTL_TERM / (5.0 * pressure * temperature)
        c_terms[t, 0] = mean[0]
        c_terms[t, 1] = inverse
        c_terms[t, 2] = factor * heat[0]
        c_terms[t, 3] = DT * rate * density * jnp.exp(-1.5 * log_t)
        c_terms[t, 4] = 1.0 - DT * rate
        for b in range(NV):
            c = node(b)
            width = c - mean[1]
            square = width * width * inverse
            at = pl.ds(b * 8, 8)
            b_terms[t, 0, at, :] = jnp.exp(-0.5 * square)
            b_terms[t, 1, at, :] = factor * heat[1] * width
            b_terms[t, 2, at, :] = square
            b_terms[t, 3, at, :] = (DT * abs(c)) * ratios[t, 3 if c < 0 else 2]
        for eh in range(2):
            width = nodes[eh] - mean[2]
            square = width * width * inverse
            e_terms[t, 0, eh] = jnp.exp(-0.5 * square)
            e_terms[t, 1, eh] = factor * heat[2] * width
            e_terms[t, 2, eh] = square - 5.0
            e_terms[t, 3, eh] = (DT * jnp.abs(nodes[eh])) * ratios[t, 5 if eh == 0 else 4]

    def advance_plane(s, t, p, plane):
        for g in range(4):
            @pl.when(remote(t, g))
            def _(g=g):
                _, device, _ = block(t, OFFSETS[g])
                pltpu.make_async_remote_copy(
                    src_ref=send_buf.at[s, t, p, g], dst_ref=recv_buf.at[s, t, p, g],
                    send_sem=send_sem.at[s, t, p, g], recv_sem=recv_sem.at[s, t, p, g],
                    device_id={"cell": device},
                ).wait_recv()
        pieces = [plane]
        for pair in range(2):
            first, second = recv_buf[s, t, p, 2 * pair], recv_buf[s, t, p, 2 * pair + 1]
            pieces.append(jnp.concatenate([
                jnp.where(low_lanes, first, pltpu.roll(second, 64, 1)),
                jnp.where(low_lanes, pltpu.roll(first, 64, 1), second),
            ], 0))
        high, low = split(jnp.concatenate(pieces, 1))

        def across(k, spans):
            left = jnp.concatenate([h[i:j] for h in (high, low) for i, j in spans], 0)
            both = jnp.dot(left, move[t, k], preferred_element_type=F32)
            size = both.shape[0] // 2
            return both[:size] + both[size:]

        xs = across(0, [(0, 256)])
        ys = [across(1, [(0, 64), (128, 192)]), across(2, [(64, 128), (192, 256)])]
        zs = [across(3, [(0, 128)]), across(4, [(128, 256)])]
        live = live_cells(t)
        c = node((first_a + p).astype(F32))
        speed = DT * jnp.abs(c)
        width = c - c_terms[t, 0]
        square = width * width * c_terms[t, 1]
        a_gauss = c_terms[t, 3] * jnp.exp(-0.5 * square)
        a_heat = c_terms[t, 2] * width
        a_keep = c_terms[t, 4] - speed * ratios[t, 0]
        rows = []
        for eh in range(2):
            e_speed = DT * jnp.abs(nodes[eh])
            gauss = a_gauss * e_terms[t, 0, eh]
            warm = a_heat + e_terms[t, 1, eh]
            shape = square + e_terms[t, 2, eh]
            keep = a_keep - e_terms[t, 3, eh]
            for b in range(NV):
                at = eh * 128 + b * 8
                bs = pl.ds(b * 8, 8)
                iy = (b % 8) * 8 + 64 * eh
                f = plane[at:at + 8]
                shakhov = gauss * b_terms[t, 0, bs, :] * (
                    1.0 + (warm + b_terms[t, 1, bs, :]) * (shape + b_terms[t, 2, bs, :])
                )
                new = f * (keep - b_terms[t, 3, bs, :]) + shakhov
                new = new + speed * xs[at:at + 8]
                new = new + (DT * abs(node(b))) * ys[b // 8][iy:iy + 8]
                new = new + e_speed * zs[eh][b * 8:b * 8 + 8]
                rows.append(jnp.where(live, new, 0.0))
        return jnp.concatenate(rows, 0)

    def load(ref, p):
        return jnp.concatenate([ref[p, :, eh].reshape(128, 256) for eh in range(2)], 0)

    def store(ref, p, new):
        for eh in range(2):
            ref[p, :, eh] = new[eh * 128:eh * 128 + 128].reshape(16, 8, 256)

    meta[x] = meta_in[...]
    matrices(x)

    def first_send(p, carry):
        send_plane(0, x, p, load(dist, x * half + p))
        return carry

    lax.fori_loop(0, half, first_send, 0)
    acc[...] = jnp.zeros_like(acc)

    def first_moments(p, carry):
        add_moments(x, base + p, load(dist, p))
        return carry

    lax.fori_loop(0, planes, first_moments, 0)
    reduce_moments(0, x)
    part[0, other] = jnp.zeros((16, 256), F32)
    for k in range(1, 2 * n_vel):
        part_copy(0, k).start()
    acc[...] = jnp.zeros_like(acc)

    def rest_of_bulk(p, carry):
        bulk_copy(p).start()
        return carry

    lax.fori_loop(1, half, rest_of_bulk, 0)
    meta_copy.wait()
    matrices(other)

    for t in range(2):
        for g in range(4):
            inside, _, _ = block(t, OFFSETS[g])

            @pl.when(jnp.logical_not(inside))
            def _(t=t, g=g):
                for s in range(STEPS):
                    def clear(p, carry):
                        recv_buf[s, t, p, g] = jnp.zeros((128, 128), F32)
                        return carry
                    lax.fori_loop(0, half, clear, 0)

    for k in range(1, 2 * n_vel):
        part_copy(0, k).wait()

    def both_terms(s):
        def one(t, carry):
            terms(s, t)
            return carry
        lax.fori_loop(0, 2, one, 0)

    both_terms(0)

    def first_advance(t, p, plane):
        new = advance_plane(0, t, p, plane)
        send_plane(1, t, p, new)
        state1[t, p] = new
        add_moments(t, first_a + p, new)

    def first_step(p, carry):
        @pl.when(p < half)
        def _():
            bulk_copy(p).wait_recv()
            send_plane(0, other, p, load(bulk, p))

        @pl.when(p > 0)
        def _():
            first_advance(x, p - 1, load(dist, x * half + p - 1))
            first_advance(other, p - 1, load(bulk, p - 1))
        return carry

    lax.fori_loop(0, half + 1, first_step, 0)

    def both_reduce(t, carry):
        reduce_moments(1, t)
        return carry

    lax.fori_loop(0, 2, both_reduce, 0)
    for k in range(1, 2 * n_vel):
        part_copy(1, k).start()
    for k in range(1, 2 * n_vel):
        part_copy(1, k).wait()
    both_terms(1)

    def second_other(p, carry):
        store(out_buf, p, advance_plane(1, other, p, state1[other, p]))
        out_copy(p).start()
        return carry

    lax.fori_loop(0, half, second_other, 0)

    def second_own(p, carry):
        store(out, x * half + p, advance_plane(1, x, p, state1[x, p]))
        return carry

    lax.fori_loop(0, half, second_own, 0)

    def drain(p, carry):
        bulk_copy(p).wait_send()
        for s in range(STEPS):
            for t in range(2):
                for j in range(4):
                    if (t, j) not in ((1, 0), (0, 3)):
                        inside, _, _ = block(t, OFFSETS[j])

                        @pl.when(inside)
                        def _(s=s, t=t, j=j):
                            message(s, t, p, j).wait_send()
        out_copy(p).wait()
        return carry

    lax.fori_loop(0, half, drain, 0)


def solution(mesh):
    n_cell, n_vel = mesh.shape["cell"], mesh.shape["vel"]

    def body(distribution, cell_count, cell_level, send_list, face_neighbour, face_level):
        rows, width = distribution.shape
        planes = rows // (NV * NV)
        shape = (planes, NV, 2, NV // 2, width)
        half = planes // 2
        vmem = pl.BlockSpec(memory_space=pltpu.VMEM)
        meta = jnp.concatenate([
            face_neighbour, face_level, cell_level.reshape(1, width), send_list.reshape(1, width),
            jnp.broadcast_to(cell_count.reshape(1, 1), (2, width)),
        ], 0)
        result = pl.pallas_call(
            functools.partial(kernel, n_cell, n_vel, planes),
            out_shape=jax.ShapeDtypeStruct(shape, F32),
            in_specs=[vmem, vmem],
            out_specs=vmem,
            scratch_shapes=[
                pltpu.VMEM((2, 16, 256), jnp.int32),
                pltpu.VMEM((half, NV, 2, NV // 2, width), F32),
                pltpu.VMEM((half, NV, 2, NV // 2, width), F32),
                pltpu.VMEM((2, half, 256, 256), F32),
                pltpu.VMEM((STEPS, 2, half, 4, 128, 128), F32),
                pltpu.VMEM((STEPS, 2, half, 4, 128, 128), F32),
                pltpu.VMEM((2, 256, 256), BF16),
                pltpu.VMEM((2, 5, 512, 256), BF16),
                pltpu.VMEM((2, 4, 256, 256), F32),
                pltpu.VMEM((STEPS, 2, 16, 256), F32),
                pltpu.VMEM((STEPS, 2 * n_vel, 2, 16, 256), F32),
                pltpu.VMEM((2, 4, 128, 256), F32),
                pltpu.VMEM((2, 4, 2, 8, 256), F32),
                pltpu.VMEM((2, 5, 8, 256), F32),
                pltpu.VMEM((2, 6, 8, 256), F32),
                pltpu.SemaphoreType.DMA((STEPS, 2, half, 4)),
                pltpu.SemaphoreType.DMA((STEPS, 2, half, 4)),
                pltpu.SemaphoreType.DMA((STEPS, 2 * n_vel)),
                pltpu.SemaphoreType.DMA((STEPS, 2 * n_vel)),
                pltpu.SemaphoreType.DMA((half,)),
                pltpu.SemaphoreType.DMA((half,)),
                pltpu.SemaphoreType.DMA((half,)),
                pltpu.SemaphoreType.DMA((half,)),
                pltpu.SemaphoreType.DMA,
                pltpu.SemaphoreType.DMA,
            ],
            compiler_params=pltpu.CompilerParams(
                collective_id=0, has_side_effects=True, vmem_limit_bytes=48 * 2**20
            ),
        )(distribution.reshape(shape), meta)
        return result.reshape(rows, width)

    placed = (P("vel", "cell"), P("cell"), P("cell"), P(None, "cell"), P(None, "cell"), P(None, "cell"))
    return jax.shard_map(body, mesh=mesh, in_specs=placed, out_specs=P("vel", "cell"), check_vma=False)
```

time: 80.3 us -> 73.5 us (0.915)
  the two profiles are of different devices: /device:TPU:13 before, /device:TPU:0 now
where the time goes in v2:
time: 73.5 us; the launch traced here: 73.1 us
  Pallas kernels  66.6 us (91%)
  local copies, waits for them, and re-layouts  5.85 us (8%)
    pallas_call x1, Pallas kernels, body(): pl.pallas_call(functools.partial(kernel, n_cell, n_vel, planes), out_shap...  66.6 us
    unnamed x3, local copies, waits for them, and re-layouts  2.91 us
    concatenate x1, local copies, waits for them, and re-layouts, body(): jnp.concatenate([face_neighbour, face_level, cell_level.reshape(1, width)...  2.18 us

profile of v2, /device:TPU:0, one launch (start us, length us, event | category | flops | bytes accessed | tf_op | source)
XLA Modules:
  0.0 73.1 jit_solution(8073385624635575175)
XLA Ops:
  0.7 0.8 %reshape.16 = s32[1,256]{1,0:T(1,128)S(1)} reshape(s32[4,64]{1,0:T(4,128)} %param.9) | data formatting | bytes 2048 | tf_op jit(solution)/shard_map/reshape | solution.py:449
  1.4 2.2 %concatenate.3.meta_in = s32[16,256]{1,0:T(8,128)S(1)} concatenate(s32[6,256]{1,0:T(8,128)} %param.10, s32[6,256]{1,0:T(8,128)} %param.11, s32[1,256]{1,0:T(1,128)} %bitcast.7, s32[1,256]{1,0:T(1,128)S(1)} %reshape.16, s32[2,256]{1,0:T(2,128)S(1)} %broadcast_in_dim.8), dimensions={0} | concatenate | bytes 32768 | tf_op jit(solution)/shard_map/concatenate | solution.py:448
  3.6 0.0 copy-start
  3.6 1.6 %copy-done = f32[2048,256]{1,0:T(8,128)S(1)} copy-done((f32[2048,256]{1,0:T(8,128)S(1)}, f32[2048,256]{1,0:T(8,128)}, u32[]{:S(2)}) %copy-start) | copy-done | bytes 2097176
  5.2 66.6 %shard_map.64 = f32[8,16,2,8,256]{4,3,2,1,0:T(8,128)S(1)} custom-call(f32[8,16,2,8,256]{4,3,2,1,0:T(8,128)S(1)} %bitcast.6, s32[16,256]{1,0:T(8,128)S(1)} %concatenate.3.meta_in), custom_call_target="tpu_custom_call" | custom-call | tf_op jit(solution)/shard_map/pallas_call | solution.py:452
  71.8 1.3 %copy.9 = f32[2048,256]{1,0:T(8,128)} copy(f32[2048,256]{1,0:T(8,128)S(1)} %bitcast.5) | data formatting | bytes 4194304
  (1 shorter events, 0.0 us)
Async XLA Ops:
  3.6 1.6 %copy-start = (f32[2048,256]{1,0:T(8,128)S(1)}, f32[2048,256]{1,0:T(8,128)}, u32[]{:S(2)}) copy-start(f32[2048,256]{1,0:T(8,128)} %param.6) | copy-start | bytes 6291460
